TPU v7x, 256 devices: a whole 4x4x8 slice. The times are simulated.
256 devices in a mesh: leaf: 256 (over y, z, x, core).
Axes of the slice: x: 4, y: 4, z: 8, core: 2. Of those that a mesh axis runs over, the one named last changes fastest.
Arguments:
- measured: bfloat16 [16, 1048576], P(None, 'leaf'), may hold values from -6 to 6
- cluster_perm: int32 [256, 4096], P('leaf'), may hold values from 0 to 4095, each once within a row
- near_offsets: int32 [16384, 4], P('leaf'), may hold values from -2 to 2
- near_blocks: bfloat16 [16384, 64, 256], P('leaf'), may hold values from -0.375 to 0.375
- leaf_bases: bfloat16 [16384, 4096], P('leaf'), may hold values from -0.75 to 0.75
- local_transfer: bfloat16 [16128, 64, 128], P('leaf'), may hold values from -0.5 to 0.5
- coupling_pattern: int32 [32256, 2], P('leaf'), may hold values from 2 to 127, as said below
- local_coupling: bfloat16 [32256, 64, 128], P('leaf'), as said below
- root_transfer: bfloat16 [256, 4096], P('leaf'), may hold values from -0.5 to 0.5
- top_blocks: bfloat16 [256, 64, 128], replicated, as said below
Outputs:
- covariance_product: float32 [16, 1048576], P(None, 'leaf')
Inputs may be any that keep to these rules, and one draw needn't show every extreme that they name: `coupling_pattern`: row d * 126 + s - 2 belongs to slot s of subtree d; its entries are other slots of the same depth in that subtree. `local_coupling`: coupling blocks of the slots of each subtree in heap order. `top_blocks`: row 0 and the transfer half of row 1 are not used.
All inputs are finite; a program needn't handle non-finite values.
Results may differ from a plain program's by a relative error of at most 0.00065.
Values may be sent and summed in bfloat16 or wider, within the bound.
A program may use at most 128 MiB of HBM per device.

v0:
```python
import jax
import jax.numpy as jnp
from jax import lax
from jax.experimental import pallas as pl
from jax.experimental.pallas import tpu as pltpu
from jax.sharding import PartitionSpec as P

F32 = jnp.float32
BF16 = jnp.bfloat16
MESH = pl.DeviceIdType.MESH
NRHS = 16
RANK = 64
LEAVES = 64
POINTS = 4096
SPAN = 256
CHUNKS = POINTS // SPAN
COARSE = POINTS // SPAN

UP_SLOT = {4: 0, 3: 16, 2: 24, 7: 28, 6: 32, 5: 34}
UP_COUNT = {4: 16, 3: 8, 2: 4, 7: 4, 6: 2, 5: 1}

NEAR_PEERS = (4, 5, 6, 7, 2, 3, 1)
Z_HOPS = (0, 1, 2, 3, 4, 3, 2, 3)
Y_HOPS = (0, 1, 2, 1)
FAR_PEERS = tuple(sorted(range(1, 32), key=lambda k: -Z_HOPS[k % 8] - Y_HOPS[k // 8]))


def nn(a, b):
    return lax.dot_general(a, b, (((1,), (0,)), ((), ())), preferred_element_type=F32)


def nt(a, b):
    return lax.dot_general(a, b, (((1,), (1,)), ((), ())), preferred_element_type=F32)


def flipped(index, mask):
    out = index
    for bit in range(8):
        if (mask >> bit) & 1:
            step = 1 << bit
            out = out + step * (1 - 2 * lax.rem(lax.div(index, step), 2))
    return out


def split(x):
    high = x.astype(BF16)
    return high, (x - high.astype(F32)).astype(BF16)


def stacked(x):
    return jnp.concatenate(split(x), axis=0)[:, :RANK]


def folded(x):
    return x[0:NRHS] + x[NRHS : 2 * NRHS]


def swapped(x):
    return pltpu.roll(x, RANK, axis=1)


def kernel(
    offsets_hbm,
    pattern_hbm,
    measured_hbm,
    perm_hbm,
    near_hbm,
    bases_hbm,
    transfer_hbm,
    coupling_hbm,
    root_hbm,
    top_hbm,
    out,
    offsets,
    pattern,
    measured,
    perm,
    near_blocks,
    bases,
    transfer,
    coupling,
    root_row,
    tops,
    climbs,
    group_up,
    local_map,
    up_map,
    reach,
    root_rows,
    root_wide,
    perm_rows,
    mix,
    mixed_order,
    mixed_points,
    basis,
    basis_pairs,
    onehot,
    points,
    coef,
    local_terms,
    near_part,
    fields,
    combined,
    edges,
    halo,
    first,
    first_coef,
    second,
    second_coef,
    in_sem,
    top_sem,
    send_sem,
    recv_sem,
    ready,
):
    me = lax.axis_index("leaf")
    right = lax.rem(me + 1, 256)
    left = lax.rem(me + 255, 256)
    low = lax.broadcasted_iota(jnp.int32, (NRHS, 128), 1) < RANK

    loads = [
        pltpu.make_async_copy(source, target, in_sem.at[i])
        for i, (source, target) in enumerate(
            [
                (perm_hbm, perm),
                (measured_hbm, measured),
                (bases_hbm, bases),
                (root_hbm, root_row),
                (transfer_hbm, transfer),
                (coupling_hbm, coupling),
                (near_hbm, near_blocks),
                (pattern_hbm, pattern),
                (offsets_hbm, offsets),
            ]
        )
    ]
    for load in loads[:4]:
        load.start()

    barrier = pltpu.get_barrier_semaphore()
    core = lax.rem(me, 2)
    place = lax.rem(me, 8)

    def tell(device):
        pl.semaphore_signal(barrier, inc=1, device_id=(device,), device_id_type=MESH)

    @pl.when(place == 7)
    def _():
        tell(right)

    @pl.when(place == 0)
    def _():
        tell(left)

    for k in (4, 2, 6):
        tell(flipped(me - core, k))

    @pl.when(core == 1)
    def _():
        tell(me - 1)

    for k in FAR_PEERS:
        tell(flipped(me - core + 1, 8 * k))

    loads[4].start()
    natural = lax.broadcasted_iota(jnp.int32, (SPAN, SPAN), 0)
    column = lax.broadcasted_iota(jnp.int32, (SPAN, SPAN), 1)
    within = lax.rem(column, RANK)
    wanted = column - within + 2 * lax.rem(within, 32) + lax.div(within, 32)
    mix[...] = jnp.where(natural == wanted, 1.0, 0.0).astype(BF16)
    loads[0].wait()
    for c in range(CHUNKS):
        perm_rows[c : c + 1, :] = perm[0:1, c * SPAN : (c + 1) * SPAN]
    order = perm_rows[...]
    digits = jnp.concatenate([lax.rem(order, SPAN), lax.div(order, SPAN)], axis=0)
    mixed = nn(digits.astype(F32).astype(BF16), mix[...])
    mixed_order[...] = mixed.astype(jnp.int32)
    fine_order = mixed.astype(BF16)
    numbers = natural.astype(F32).astype(BF16)
    one, zero = jnp.ones((SPAN, SPAN), BF16), jnp.zeros((SPAN, SPAN), BF16)

    loads[1].wait()
    loads[2].wait()
    loads[3].wait()
    group = lax.div(me, 8)
    top_loads = [
        pltpu.make_async_copy(top_hbm.at[pl.ds(start, count)], tops.at[pl.ds(at, count)], top_sem.at[0])
        for start, at, count in (
            (0, 0, 32),
            (32 + group, 32, 1),
            (64 + 2 * group, 33, 2),
            (128 + 4 * group, 35, 4),
        )
    ]
    for load in top_loads:
        load.start()
    for load in loads[5:]:
        load.start()
    for pair in range(32):
        root_rows[pair : pair + 1, :] = root_row[0:1, pair * 128 : (pair + 1) * 128].astype(F32)
    both = root_rows[...]
    turned = swapped(both)
    low_half = lax.broadcasted_iota(jnp.int32, (32, 128), 1) < RANK
    root_wide[pl.ds(0, 32, stride=2), :] = jnp.where(low_half, both, turned)
    root_wide[pl.ds(1, 32, stride=2), :] = jnp.where(low_half, turned, both)
    root_map = root_wide[...].astype(BF16)

    spread = jnp.concatenate(
        [measured[:, h * SPAN : (h + 1) * SPAN] for h in range(COARSE)], axis=0
    )
    for c in range(CHUNKS):
        at = slice(c * SPAN, (c + 1) * SPAN)
        hot = jnp.where(numbers == fine_order[c : c + 1, :], one, zero)
        onehot[:, at] = hot
        picked = nn(spread, hot)
        coarse = jnp.broadcast_to(mixed_order[COARSE + c : COARSE + c + 1, :], (NRHS, SPAN))
        chosen = picked[0:NRHS]
        for h in range(1, COARSE):
            chosen = jnp.where(coarse == h, picked[h * NRHS : (h + 1) * NRHS], chosen)
        mixed_points[:, at] = chosen.astype(BF16)

    loads[4].wait()
    low_rank = lax.broadcasted_iota(jnp.int32, (RANK, 128), 1) < RANK

    def opened(x):
        return x + swapped(x)

    def both_parts(x):
        high = x.astype(BF16).astype(F32)
        return jnp.where(low_rank, high, x - high).astype(BF16)

    def folded_rows(x):
        return x[0:RANK] + x[RANK : 2 * RANK]

    first_pair = transfer[0].astype(F32)
    maps = {
        2: jnp.where(low_rank, first_pair, 0.0).astype(BF16),
        3: jnp.where(low_rank, swapped(first_pair), 0.0).astype(BF16),
    }
    products = {}

    def multiply(slot):
        block = transfer[slot // 2 - 1]
        step = block[:, :RANK] if slot % 2 == 0 else block[:, RANK:]
        products[slot] = opened(nn(step, maps[slot // 2]))
        maps[slot] = both_parts(products[slot])
        if slot >= 16:
            local_map[slot - 16] = maps[slot]

    def through_root(slot):
        rows = jnp.concatenate(split(products[slot]), axis=0)[:, :RANK]
        up_map[slot - 8] = both_parts(folded_rows(nn(rows, root_map)))

    tasks = [(multiply, slot) for slot in range(4, 16)] + [(through_root, slot) for slot in range(8, 16)]

    turn = jnp.where(lax.rem(natural, 8) * 32 + lax.div(natural, 8) == column, 1.0, 0.0).astype(BF16)
    low_half = lax.broadcasted_iota(jnp.int32, (32, 128), 1) < RANK
    for side in range(2):
        rows = slice(side * 32, (side + 1) * 32)
        blocks = []
        for eight in range(4):
            taken = [bases[rows, (8 * eight + k) * 128 : (8 * eight + k + 1) * 128] for k in range(8)]
            blocks.append(nn(turn, jnp.concatenate(taken, axis=0)))
        for leaf in range(32):
            both = jnp.concatenate([block[leaf * 8 : (leaf + 1) * 8] for block in blocks], axis=0)
            turned = swapped(both)
            at = (side * 32 + leaf) * RANK
            basis[at : at + RANK, :] = jnp.concatenate(
                [jnp.where(low_half, both, turned), jnp.where(low_half, turned, both)], axis=0
            ).astype(BF16)
            if leaf % 3 == 0 and tasks:
                task, slot = tasks.pop(0)
                task(slot)

    quarter = lax.broadcasted_iota(jnp.int32, (NRHS, 256), 1) // RANK
    for four in range(LEAVES // 4):
        chunk = mixed_points[:, four * SPAN : (four + 1) * SPAN].astype(F32)
        block = jnp.concatenate(
            [jnp.where(quarter == k, chunk, 0.0) for k in range(4)], axis=0
        ).astype(BF16)
        result = nn(block, basis[four * 256 : (four + 1) * 256, :])
        for k in range(4):
            coef[64 + 4 * four + k] = jnp.concatenate(
                split(result[k * NRHS : (k + 1) * NRHS]), axis=0
            )

    def climb(parent):
        children = coef[pl.ds(2 * parent, 2)].reshape(64, 128)[:, :RANK]
        result = nn(children, transfer[parent - 1])
        mixed = jnp.where(low, folded(result[0:32]), folded(result[32:64]))
        return mixed + swapped(mixed)

    def climb_levels(levels):
        for level in levels:
            values = []
            for parent in range(1 << level, 2 << level):
                values.append(climb(parent))
                coef[parent] = jnp.concatenate(split(values[-1]), axis=0)
        return values

    def pairs_of(values):
        wide = [jnp.where(low, values[k], values[k + 1]) for k in range(0, len(values), 2)]
        return jnp.concatenate(split(jnp.concatenate(wide, axis=1)), axis=0)

    depth_3 = climb_levels((5, 4, 3))
    root_up = opened(folded(nn(pairs_of(depth_3), up_map[...].reshape(512, 128))))

    def packed(x):
        high = x.astype(BF16).astype(F32)
        return jnp.where(low, high, x - high).astype(BF16)

    def send(buffer, slot, mask, at):
        copy = pltpu.make_async_remote_copy(
            src_ref=buffer.at[0],
            dst_ref=buffer.at[slot],
            send_sem=send_sem.at[at],
            recv_sem=recv_sem.at[at],
            device_id=(flipped(me, mask),),
            device_id_type=MESH,
        )
        copy.start()

    def arrived(buffer, at):
        slots = buffer.at[pl.ds(1, buffer.shape[0] - 1)]
        pltpu.make_async_remote_copy(
            src_ref=slots,
            dst_ref=slots,
            send_sem=send_sem.at[at],
            recv_sem=recv_sem.at[at],
            device_id=(flipped(me, 1),),
            device_id_type=MESH,
        ).wait()

    first[0] = packed(root_up)

    def tell_other_core(at):
        pl.semaphore_signal(ready.at[at], inc=1, device_id=(flipped(me, 1),), device_id_type=MESH)

    @pl.when(core == 0)
    def _():
        pl.semaphore_wait(barrier, 7 + lax.div(7 - place, 7))
        tell_other_core(0)

    @pl.when(core == 1)
    def _():
        pl.semaphore_wait(ready.at[0], 1)

    for k in NEAR_PEERS:
        send(first, k, k, 0)
    @pl.when(core == 1)
    def _():
        pl.semaphore_wait(barrier, 62 + lax.div(place, 7))
        tell_other_core(1)

    for slot in range(16, 32):
        multiply(slot)
    climb_levels((2, 1))
    first_coef[0] = packed(climb(1))
    send(first_coef, 1, 1, 1)

    pltpu.make_async_copy(top_hbm.at[pl.ds(0, 39)], tops, top_sem.at[0]).wait()

    def top_row(level, k):
        if level == 0:
            return 1
        own = lax.div(me, 1 << (8 - level))
        if level < 5:
            return (1 << level) + flipped(own, k)
        if level == 5:
            return 32
        return (33 if level == 6 else 35) + flipped(lax.rem(own, 1 << (level - 5)), k)

    for level, count in UP_COUNT.items():
        for k in range(count):
            block = tops[top_row(level, k)].astype(F32)
            climbs[UP_SLOT[level] + k] = jnp.where(low_rank, swapped(block), block).astype(BF16)

    unmixed = nt(
        jnp.concatenate(
            [mixed_points[:, c * SPAN : (c + 1) * SPAN] for c in range(CHUNKS)], axis=0
        ),
        mix[...],
    )
    for m in range(LEAVES // 2):
        c, pair = m // 2, m % 2
        both = unmixed[c * NRHS : (c + 1) * NRHS, pair * 128 : (pair + 1) * 128]
        turned = swapped(both)
        points[2 * m + 2] = jnp.where(low, both, turned).astype(BF16)
        points[2 * m + 3] = jnp.where(low, turned, both).astype(BF16)
        if m == 0:
            edges[0] = both.astype(BF16)
        if m == LEAVES // 2 - 1:
            edges[1] = both.astype(BF16)

    halo_copies = [
        pltpu.make_async_remote_copy(
            src_ref=edges.at[side],
            dst_ref=halo.at[side],
            send_sem=send_sem.at[4],
            recv_sem=recv_sem.at[4],
            device_id=(target,),
            device_id_type=MESH,
        )
        for side, target in ((0, left), (1, right))
    ]
    for copy in halo_copies:
        copy.start()


    def couple(pair):
        sides = []
        for k in range(2):
            n = 2 * pair + k
            sides.append(
                jnp.concatenate(
                    [coef[pattern[0, n]][:, :RANK], coef[pattern[1, n]][:, RANK:]], axis=1
                )
            )
        blocks = coupling[pl.ds(2 * pair, 2)].reshape(128, 128)
        result = nt(jnp.concatenate(sides, axis=0), blocks)
        local_terms[pair + 1] = jnp.where(low, folded(result[0:32]), folded(result[32:64]))

    def near(pair):
        sides = []
        for k in range(2):
            leaf = 2 * pair + k
            at = [points[leaf + 2 + offsets[j, leaf]] for j in range(4)]
            sides.append(
                jnp.concatenate(
                    [at[0][:, :RANK], at[1][:, RANK:], at[2][:, :RANK], at[3][:, RANK:]], axis=1
                )
            )
        blocks = near_blocks[pl.ds(2 * pair, 2)].reshape(128, 256)
        result = nt(jnp.concatenate(sides, axis=0), blocks)
        near_part[pair] = jnp.where(low, result[0:NRHS], result[NRHS : 2 * NRHS])

    def lift(values, level):
        out = []
        for k in range(0, len(values), 2):
            both = jnp.where(low, values[k], values[k + 1])
            blocks = climbs[pl.ds(UP_SLOT[level] + k, 2)].reshape(128, 128)
            out.append(folded(nn(jnp.concatenate(split(both), axis=0), blocks)))
        return out

    def coupled(sibling, level):
        block = tops[top_row(level - 1, 0)]
        parts = stacked(sibling)
        to_left = folded(nt(parts, block[:, :RANK]))
        to_right = folded(nn(parts, block))[:, :RANK]
        odd = lax.rem(lax.div(me, 1 << (8 - level)), 2)
        return jnp.where(odd == 1, to_right, to_left)

    def received(buffer, k):
        return opened(buffer[k].astype(F32) + buffer[k + 1].astype(F32))

    for side in range(2):
        inner = split(nn(climbs[UP_SLOT[6] + side][:, :RANK], climbs[UP_SLOT[5]]))
        for k in (2 * side, 2 * side + 1):
            outer = climbs[UP_SLOT[7] + k][:, :RANK]
            high, rest = split(nn(outer, inner[0]) + nn(outer, inner[1]))
            group_up[k * RANK : (k + 1) * RANK, :] = jnp.where(
                low_rank, high.astype(F32), rest.astype(F32)
            ).astype(BF16)

    terms = {}
    arrived(first, 0)
    at_7 = [received(first, 2 * k) for k in range(4)]
    second[0] = packed(opened(folded(nn(pairs_of(at_7), group_up[...]))))

    @pl.when(core == 0)
    def _():
        pl.semaphore_wait(ready.at[1], 1)

    for k in FAR_PEERS:
        send(second, k, 8 * k, 2)
    at_6 = lift(at_7, 7)
    at_5 = lift(at_6, 6)[0]
    second_coef[0] = packed(at_5)
    send(second_coef, 1, 8, 3)
    def stacked_rows(x):
        return jnp.concatenate(split(x), axis=0)

    def times(x, block):
        return folded_rows(nn(stacked_rows(x), block))

    def times_turned(x, blocks):
        return folded_rows(nt(stacked_rows(x), blocks))

    def outward(x, level, k):
        blocks = climbs[pl.ds(UP_SLOT[level] + k, 2)].reshape(128, 128)[:, :RANK]
        return times_turned(x, blocks)

    def halves(x):
        return [x[:, :RANK], swapped(x)[:, :RANK]]

    down = {7: root_map[:, :RANK].astype(F32)}
    for level in range(6, 0, -1):
        down[level] = times(down[level + 1], climbs[UP_SLOT[level + 1]])[:, :RANK]

    def crossing(level):
        block = tops[top_row(level - 1, 0)]
        to_left = times(down[level], block)[:, :RANK]
        to_right = times_turned(down[level], block[:, :RANK])
        odd = lax.rem(lax.div(me, 1 << (8 - level)), 2)
        return jnp.where(odd == 1, to_right, to_left)

    by_pair = [jnp.concatenate([jnp.zeros((RANK, RANK), F32), crossing(4)], axis=1)]
    by_pair.append(outward(crossing(3), 4, 2))
    for j, part in enumerate(halves(outward(crossing(2), 3, 2))):
        by_pair.append(outward(part, 4, 4 + 2 * j))
    for i, outer in enumerate(halves(outward(crossing(1), 2, 2))):
        for j, part in enumerate(halves(outward(outer, 3, 4 + 2 * i))):
            by_pair.append(outward(part, 4, 8 + 4 * i + 2 * j))
    for p in range(8):
        reach[:, p * 128 : (p + 1) * 128] = stacked_rows(by_pair[p])

    arrived(first_coef, 1)
    terms[8] = coupled(opened(first_coef[1].astype(F32)), 8)
    terms[7] = coupled(at_7[1], 7)
    terms[6] = coupled(at_6[1], 6)

    for m in range(32):
        basis_pairs[m] = jnp.where(
            low_rank,
            basis[m * 128 : m * 128 + RANK, :].astype(F32),
            basis[m * 128 + RANK : (m + 1) * 128, :].astype(F32),
        ).astype(BF16)

    loads[5].wait()
    loads[7].wait()

    @pl.loop(0, 9)
    def _(step):
        for k in range(7):
            couple(7 * step + k)

    pltpu.make_async_remote_copy(
        src_ref=edges,
        dst_ref=halo,
        send_sem=send_sem.at[4],
        recv_sem=recv_sem.at[4],
        device_id=(left,),
        device_id_type=MESH,
    ).wait()
    for side, leaf, end in ((1, 0, 0), (0, 66, 255)):
        both = jnp.where(me == end, 0.0, halo[side].astype(F32))
        turned = swapped(both)
        points[leaf] = jnp.where(low, both, turned).astype(BF16)
        points[leaf + 1] = jnp.where(low, turned, both).astype(BF16)
    loads[6].wait()
    loads[8].wait()

    @pl.loop(0, 4)
    def _(step):
        for k in range(8):
            near(8 * step + k)

    arrived(second_coef, 3)
    def descend(parent, here, there):
        lhs = jnp.concatenate(
            [jnp.where(low, part, 0.0) for part in here]
            + [jnp.where(low, 0.0, part) for part in there],
            axis=0,
        ).astype(BF16)
        result = nt(lhs, transfer[parent - 1])
        fields[parent] = local_terms[parent] + side_by_side(result)

    def side_by_side(result):
        return jnp.concatenate([folded(result[0:32]), folded(result[32:64])], axis=1)

    def parts_of(x):
        high = x.astype(BF16).astype(F32)
        return high, x - high

    def descend_levels(levels):
        for level in levels:
            for q in range(1 << level, 2 << level):
                pair = fields[q]
                straight = parts_of(pair)
                crossed = parts_of(swapped(pair))
                descend(2 * q, straight, crossed)
                descend(2 * q + 1, crossed, straight)

    fields[1] = local_terms[1]
    descend_levels((0, 1, 2))

    naturals = jnp.concatenate([near_part[m] for m in range(LEAVES // 2)], axis=0)
    high, rest = split(naturals)
    mixer = mix[0:128, 0:128]
    turned = nn(high, mixer) + nn(rest, mixer)
    for m in range(LEAVES // 2):
        near_part[m] = turned[m * NRHS : (m + 1) * NRHS]

    field = coupled(opened(second_coef[1].astype(F32)), 5)
    for level in (6, 7):
        block = climbs[UP_SLOT[level]][:, :RANK]
        field = terms[level] + folded(nt(stacked(field), block))
    field = terms[8] + folded(nt(stacked(field), root_map[:, :RANK]))
    near_field = jnp.concatenate([field, field], axis=1)

    arrived(second, 2)
    at_4 = [received(second, 2 * k) for k in range(16)]
    root_field = near_field + opened(folded(nt(pairs_of(at_4), reach[...])))

    arriving = folded(
        nt(jnp.concatenate(split(root_field), axis=0), local_map[...].reshape(1024, 128))
    )
    for p in range(8, 16):
        fields[p] = fields[p] + arriving[:, (p - 8) * 128 : (p - 7) * 128]
    descend_levels((3, 4))

    for m in range(32):
        pair = fields[32 + m]
        high, rest = parts_of(pair)
        lhs = jnp.concatenate(
            [jnp.where(low, high, 0.0), jnp.where(low, rest, 0.0)]
            + [jnp.where(low, 0.0, high), jnp.where(low, 0.0, rest)],
            axis=0,
        ).astype(BF16)
        whole = near_part[m] + side_by_side(nt(lhs, basis_pairs[m]))
        combined[:, m * 128 : (m + 1) * 128] = jnp.concatenate(parts_of(whole), axis=0)

    total = jnp.zeros((COARSE * 32, SPAN), F32)
    for c in range(CHUNKS):
        at = slice(c * SPAN, (c + 1) * SPAN)
        coarse = jnp.broadcast_to(mixed_order[COARSE + c : COARSE + c + 1, :], (32, SPAN))
        values = combined[:, at]
        lhs = jnp.concatenate(
            [jnp.where(coarse == h, values, 0.0) for h in range(COARSE)], axis=0
        ).astype(BF16)
        total = total + nt(lhs, onehot[:, at])
    for h in range(COARSE):
        out[:, h * SPAN : (h + 1) * SPAN] = folded(total[h * 32 : (h + 1) * 32])


def body(
    measured,
    cluster_perm,
    near_offsets,
    near_blocks,
    leaf_bases,
    local_transfer,
    coupling_pattern,
    local_coupling,
    root_transfer,
    top_blocks,
):
    hbm = pl.BlockSpec(memory_space=pl.ANY)
    dma = pltpu.SemaphoreType.DMA
    return pl.pallas_call(
        kernel,
        out_shape=pltpu.VMEM((NRHS, POINTS), F32),
        in_specs=[hbm] * 10,
        out_specs=pl.BlockSpec(memory_space=pltpu.VMEM),
        scratch_shapes=[
            pltpu.SMEM((4, 64), jnp.int32),
            pltpu.SMEM((2, 126), jnp.int32),
            pltpu.VMEM((NRHS, POINTS), BF16),
            pltpu.VMEM((1, POINTS), jnp.int32),
            pltpu.VMEM((64, 64, 256), BF16),
            pltpu.VMEM((64, 4096), BF16),
            pltpu.VMEM((63, 64, 128), BF16),
            pltpu.VMEM((126, 64, 128), BF16),
            pltpu.VMEM((1, 4096), BF16),
            pltpu.VMEM((39, 64, 128), BF16),
            pltpu.VMEM((35, 64, 128), BF16),
            pltpu.VMEM((256, 128), BF16),
            pltpu.VMEM((16, 64, 128), BF16),
            pltpu.VMEM((8, 64, 128), BF16),
            pltpu.VMEM((128, 1024), BF16),
            pltpu.VMEM((32, 128), F32),
            pltpu.VMEM((64, 128), F32),
            pltpu.VMEM((CHUNKS, SPAN), jnp.int32),
            pltpu.VMEM((SPAN, SPAN), BF16),
            pltpu.VMEM((2 * CHUNKS, SPAN), jnp.int32),
            pltpu.VMEM((NRHS, POINTS), BF16),
            pltpu.VMEM((4096, 128), BF16),
            pltpu.VMEM((32, 64, 128), BF16),
            pltpu.VMEM((SPAN, POINTS), BF16),
            pltpu.VMEM((68, NRHS, 128), BF16),
            pltpu.VMEM((128, 2 * NRHS, 128), BF16),
            pltpu.VMEM((64, NRHS, 128), F32),
            pltpu.VMEM((32, NRHS, 128), F32),
            pltpu.VMEM((64, NRHS, 128), F32),
            pltpu.VMEM((2 * NRHS, POINTS), F32),
            pltpu.VMEM((2, NRHS, 128), BF16),
            pltpu.VMEM((2, NRHS, 128), BF16),
            pltpu.VMEM((8, NRHS, 128), BF16),
            pltpu.VMEM((2, NRHS, 128), BF16),
            pltpu.VMEM((32, NRHS, 128), BF16),
            pltpu.VMEM((2, NRHS, 128), BF16),
            dma((9,)),
            dma((1,)),
            dma((5,)),
            dma((5,)),
            pltpu.SemaphoreType.REGULAR((2,)),
        ],
        compiler_params=pltpu.CompilerParams(
            collective_id=0, has_side_effects=True, vmem_limit_bytes=57 * 1024 * 1024
        ),
    )(
        near_offsets.T,
        coupling_pattern.T,
        measured,
        cluster_perm,
        near_blocks,
        leaf_bases,
        local_transfer,
        local_coupling,
        root_transfer,
        top_blocks,
    )


def solution(mesh):
    return jax.shard_map(
        body,
        mesh=mesh,
        in_specs=(
            P(None, "leaf"),
            P("leaf", None),
            P("leaf", None),
            P("leaf", None, None),
            P("leaf", None),
            P("leaf", None, None),
            P("leaf", None),
            P("leaf", None, None),
            P("leaf", None),
            P(),
        ),
        out_specs=P(None, "leaf"),
        check_vma=False,
    )
```

profile of v0, /device:TPU:1, one launch (start us, length us, event | category | flops | bytes accessed | tf_op | source)
XLA Modules:
  0.0 25.3 jit_solution(2133881663955148036)
XLA Ops:
  0.0 24.6 %shard_map.100 = f32[16,4096]{1,0:T(8,128)S(1)} custom-call(s32[4,64]{1,0:T(4,128)} %bitcast.2, s32[2,126]{1,0:T(2,128)} %bitcast.3, bf16[16,4096]{1,0:T(8,128)(2,1)} %measured_hbm.1, s32[1,4096]{1,0:T(1,128)} %perm_hbm.1, bf16[64,64,256]{2,1,0:T(8,128)(2,1)} %near_hbm.1, bf16[64,4096]{1,0:T(8,128)(2,1)} %bases_hbm.1, bf16[63,64,128]{2,1,0:T(8,128)(2,1)} %transfer_hbm.1, ...), custom_call_target="tpu_custom_call" | custom-call | tf_op jit(solution)/shard_map/pallas_call | solution.py:650
  24.6 0.7 %copy.12 = f32[16,4096]{1,0:T(8,128)} copy(f32[16,4096]{1,0:T(8,128)S(1)} %shard_map.100) | data formatting | bytes 524288
where the time goes:
time: 25.4 us; the launch traced here: 25.3 us
  Pallas kernels  24.6 us (97%)
  local copies, waits for them, and re-layouts  0.71 us (3%)
    pallas_call x1, Pallas kernels, body(): pl.pallas_call(kernel, out_shape=pltpu.VMEM((NRHS, POINTS), F32), in_spec...  24.6 us
    unnamed x1, local copies, waits for them, and re-layouts  0.71 us

commit v1 on v0

--- a/solution.py
+++ b/solution.py
@@ -529,10 +529,10 @@
     loads[5].wait()
     loads[7].wait()
 
-    @pl.loop(0, 9)
+    @pl.loop(0, 3)
     def _(step):
-        for k in range(7):
-            couple(7 * step + k)
+        for k in range(21):
+            couple(21 * step + k)
 
     pltpu.make_async_remote_copy(
         src_ref=edges,
@@ -550,10 +550,10 @@
     loads[6].wait()
     loads[8].wait()
 
-    @pl.loop(0, 4)
+    @pl.loop(0, 2)
     def _(step):
-        for k in range(8):
-            near(8 * step + k)
+        for k in range(16):
+            near(16 * step + k)
 
     arrived(second_coef, 3)
     def descend(parent, here, there):

time: 25.4 us -> 25.4 us (level)
  no operation moved by 1% of the time
where the time goes in v1:
time: 25.4 us; the launch traced here: 25.3 us
  Pallas kernels  24.6 us (97%)
  local copies, waits for them, and re-layouts  0.71 us (3%)
    pallas_call x1, Pallas kernels, body(): pl.pallas_call(kernel, out_shape=pltpu.VMEM((NRHS, POINTS), F32), in_spec...  24.6 us
    unnamed x1, local copies, waits for them, and re-layouts  0.71 us

profile of v1, /device:TPU:1, one launch (start us, length us, event | category | flops | bytes accessed | tf_op | source)
XLA Modules:
  0.0 25.3 jit_solution(4093504101822862238)
XLA Ops:
  0.0 24.6 %shard_map.100 = f32[16,4096]{1,0:T(8,128)S(1)} custom-call(s32[4,64]{1,0:T(4,128)} %bitcast.2, s32[2,126]{1,0:T(2,128)} %bitcast.3, bf16[16,4096]{1,0:T(8,128)(2,1)} %measured_hbm.1, s32[1,4096]{1,0:T(1,128)} %perm_hbm.1, bf16[64,64,256]{2,1,0:T(8,128)(2,1)} %near_hbm.1, bf16[64,4096]{1,0:T(8,128)(2,1)} %bases_hbm.1, bf16[63,64,128]{2,1,0:T(8,128)(2,1)} %transfer_hbm.1, ...), custom_call_target="tpu_custom_call" | custom-call | tf_op jit(solution)/shard_map/pallas_call | solution.py:650
  24.6 0.7 %copy.12 = f32[16,4096]{1,0:T(8,128)} copy(f32[16,4096]{1,0:T(8,128)S(1)} %shard_map.100) | data formatting | bytes 524288
